TPU v7x, 512 devices: a whole 4x4x16 slice. The times are simulated.
512 devices in a mesh: topic: 8 (over y, core), dev: 64 (over z, x).
Axes of the slice: x: 4, y: 4, z: 16, core: 2. Of those that a mesh axis runs over, the one named last changes fastest.
Arguments:
- embeddings: bfloat16 [131072, 768], P(('topic', 'dev')), may hold values from -6 to 6
- topic_ids: int32 [131072], P(('topic', 'dev')), may hold values from 0 to 3
- pair_blocks: int32 [8, 64, 64], P('topic'), may hold values from -1 to 7, as said below
Outputs:
- smoothed: bfloat16 [131072, 768], P(('topic', 'dev'))
Inputs may be any that keep to these rules, and one draw needn't show every extreme that they name: pair_blocks[g, m, n] >= 0 exactly when pair_blocks[g, n, m] >= 0; pair_blocks[g, m, m] = -1.
All inputs are finite; a program needn't handle non-finite values.
Results may differ from a plain program's by a relative error of at most 0.0089.
Values may be sent and summed in bfloat16 or wider, within the bound.
A program may use at most 64 MiB of HBM per device.

v0:
```python
import jax
import jax.numpy as jnp
from jax import lax
from jax.sharding import PartitionSpec as P

BLOCK = 32


SHARPNESS = 60.0
LEAKAGE = 0.3
EPSILON = 1e-06


def from_behind(array, axis, by):
    count = lax.axis_size(axis)
    pairs = [(i, i + by) for i in range(count) if 0 <= i + by < count]
    return lax.ppermute(array, axis, pairs)


def normalize(embed_rows):
    values = embed_rows.astype(jnp.float32)
    row_scale = lax.rsqrt(jnp.mean(values * values, axis=-1, keepdims=True) + EPSILON)
    return (values * row_scale).astype(jnp.bfloat16)


def kernel_tiles(left_rows, right_rows, left_topic, right_topic):
    feature_width = left_rows.shape[-1]
    scores = jnp.einsum("sid,sjd->sij", left_rows, right_rows, preferred_element_type=jnp.float32)
    same_topic = left_topic[:, :, None] == right_topic[:, None, :]
    factor = jnp.where(same_topic, 1.0, LEAKAGE).astype(jnp.float32)
    return (jnp.exp(scores * (SHARPNESS / feature_width)) * factor).astype(jnp.bfloat16)


def tile_sides(my_rows, their_rows, my_topic, their_topic, live_slot):
    weights = kernel_tiles(my_rows, their_rows, my_topic, their_topic)
    weights = weights * live_slot[:, None, None].astype(jnp.bfloat16)
    wide_weights = weights.astype(jnp.float32)
    own_sum = jnp.einsum(
        "sij,sjd->sid", weights, their_rows, preferred_element_type=jnp.float32
    ).astype(jnp.bfloat16)
    own_total = jnp.sum(wide_weights, axis=2).astype(jnp.bfloat16)
    far_sum = jnp.einsum(
        "sij,sid->sjd", weights, my_rows, preferred_element_type=jnp.float32
    ).astype(jnp.bfloat16)
    far_total = jnp.sum(wide_weights, axis=1).astype(jnp.bfloat16)
    return (own_sum, own_total, far_sum, far_total)


def owned_pairs(owned, my_rows, their_rows, my_topic, their_topic):
    slot_count = owned.shape[0]
    group_size = min(8, slot_count)
    slot_order = jnp.argsort(
        jnp.where(owned, 0, slot_count).astype(jnp.int32) + jnp.arange(slot_count, dtype=jnp.int32)
    )
    owned_count = jnp.sum(owned.astype(jnp.int32))
    sorted_parts = (
        my_rows[slot_order],
        their_rows[slot_order],
        my_topic[slot_order],
        their_topic[slot_order],
        owned[slot_order],
    )
    sum_zero = jnp.zeros(my_rows.shape, jnp.bfloat16)
    total_zero = jnp.zeros(my_topic.shape, jnp.bfloat16)
    initial = (sum_zero, total_zero, sum_zero, total_zero)

    def step(step_index, carried):
        first_slot = step_index * group_size
        picked = [
            lax.dynamic_slice_in_dim(member_part, first_slot, group_size, 0)
            for member_part in sorted_parts
        ]
        results = tile_sides(picked[0], picked[1], picked[2], picked[3], picked[4])
        return tuple(
            (
                lax.dynamic_update_slice_in_dim(current, result, first_slot, 0)
                for current, result in zip(carried, results)
            )
        )

    carried = lax.fori_loop(0, (owned_count + group_size - 1) // group_size, step, initial)
    return tuple((jnp.zeros_like(current).at[slot_order].set(current) for current in carried))


def local_part(normed, topic_row):
    row_count = normed.shape[0]
    step_rows = min(512, row_count)
    weights = kernel_tiles(normed[None], normed[None], topic_row[None], topic_row[None])[0]
    own_row = 0 + jnp.arange(step_rows, dtype=jnp.int32)[:, None]
    keep_mask = own_row != jnp.arange(row_count, dtype=jnp.int32)[None, :]
    weights = jnp.where(keep_mask, weights, jnp.zeros_like(weights))
    block_sums = jnp.dot(weights, normed, preferred_element_type=jnp.float32)
    block_totals = jnp.sum(weights.astype(jnp.float32), axis=1)
    return (block_sums, block_totals)


def local(embeddings, topic_ids, pair_blocks):
    normed = normalize(embeddings)
    row_count, feature_width = normed.shape
    block_rows = BLOCK
    block_count = row_count // block_rows
    members = lax.axis_size("dev")
    member = lax.axis_index("dev")
    group_index = lax.axis_index("topic")
    topic_values = topic_ids.astype(jnp.bfloat16)
    local_sum, local_total = local_part(normed, topic_ids)
    my_blocks = pair_blocks[0][member]
    present = my_blocks >= 0
    safe_blocks = jnp.maximum(my_blocks, 0)
    blocked = normed.reshape(block_count, block_rows, feature_width)
    blocked_topic = topic_values.reshape(block_count, block_rows)
    my_rows = blocked[safe_blocks]
    my_topic = blocked_topic[safe_blocks]
    their_rows, their_topic = (
        lax.all_to_all(my_rows, "dev", split_axis=0, concat_axis=0, tiled=True),
        lax.all_to_all(my_topic, "dev", split_axis=0, concat_axis=0, tiled=True),
    )
    peers = jnp.arange(members, dtype=jnp.int32)
    first_rows = normed[:block_rows][None]
    first_topic = topic_values[:block_rows][None]
    last_rows = normed[row_count - block_rows :][None]
    last_topic = topic_values[row_count - block_rows :][None]
    previous_rows, previous_topic = from_behind((last_rows, last_topic), "topic", 1)
    has_previous = (group_index > 0)[None]
    lower_member = jnp.minimum(peers, member)
    owned = present & (lower_member == member)
    mine_sum, mine_total, far_sum, far_total = owned_pairs(
        owned, my_rows, their_rows, my_topic, their_topic
    )
    back_sum, back_total = (
        lax.all_to_all(far_sum, "dev", split_axis=0, concat_axis=0, tiled=True),
        lax.all_to_all(far_total, "dev", split_axis=0, concat_axis=0, tiled=True),
    )
    own_sum = jnp.where(owned[:, None, None], mine_sum, back_sum)
    own_total = jnp.where(owned[:, None], mine_total, back_total)
    head_sum, head_total, edge_sum, edge_total = tile_sides(
        first_rows, previous_rows, first_topic, previous_topic, has_previous
    )
    tail_sum, tail_total = from_behind((edge_sum, edge_total), "topic", -1)
    placement = (
        (my_blocks[:, None] == jnp.arange(block_count, dtype=jnp.int32)[None, :]) & present[:, None]
    ).astype(jnp.bfloat16)
    remote_sum = jnp.einsum(
        "qn,qbd->nbd", placement, own_sum, preferred_element_type=jnp.float32
    ).reshape(row_count, feature_width)
    remote_total = jnp.einsum(
        "qn,qb->nb", placement, own_total, preferred_element_type=jnp.float32
    ).reshape(row_count)
    middle_rows = row_count - 2 * block_rows
    border_sum = jnp.concatenate(
        [
            head_sum[0].astype(jnp.float32),
            jnp.zeros((middle_rows, feature_width), jnp.float32),
            tail_sum[0].astype(jnp.float32),
        ],
        0,
    )
    border_total = jnp.concatenate(
        [
            head_total[0].astype(jnp.float32),
            jnp.zeros((middle_rows,), jnp.float32),
            tail_total[0].astype(jnp.float32),
        ],
        0,
    )
    numer = local_sum + remote_sum + border_sum
    denom = local_total + remote_total + border_total
    return (numer / denom[:, None]).astype(jnp.bfloat16)


def solution(mesh):
    return jax.shard_map(
        local,
        mesh=mesh,
        in_specs=(P(("topic", "dev"), None), P(("topic", "dev")), P("topic", None, None)),
        out_specs=P(("topic", "dev"), None),
        check_vma=False,
    )
```

profile of v0, /device:TPU:24, one launch (start us, length us, event | category | flops | bytes accessed | tf_op | source)
XLA Modules:
  0.0 429.0 jit_solution(4253819287289504800)
XLA Ops:
  3.3 18.6 %all-to-all-start.1 = ((bf16[64,1,32]{2,1,0:T(2,128)(2,1)}), bf16[64,1,32]{2,1,0:T(2,128)(2,1)S(1)}, u32[]{:S(2)}, u32[]{:S(2)}) async-start(bf16[64,1,32]{2,1,0:T(2,128)(2,1)} %copy.27), calls=%async_computation.1 | async-start | bytes 65536 | tf_op jit(solution)/shard_map/all_to_all | solution.py:116
  24.1 2.4 gather_fusion
  26.5 9.8 %all-to-all-done.1 = bf16[64,1,32]{2,1,0:T(2,128)(2,1)S(1)} async-done(((bf16[64,1,32]{2,1,0:T(2,128)(2,1)}), bf16[64,1,32]{2,1,0:T(2,128)(2,1)S(1)}, u32[]{:S(2)}, u32[]{:S(2)}) %all-to-all-start.1) | async-done | bytes 4128 | tf_op jit(solution)/shard_map/all_to_all | solution.py:116
  37.0 5.3 %all-to-all-start = ((bf16[64,32,768]{2,1,0:T(8,128)(2,1)}), bf16[64,32,768]{2,1,0:T(8,128)(2,1)S(1)}, u32[]{:S(2)}, u32[]{:S(2)}) async-start(bf16[64,32,768]{2,1,0:T(8,128)(2,1)} %gather_fusion), calls=%async_computation | async-start | bytes 6291456 | tf_op jit(solution)/shard_map/all_to_all | solution.py:115
  45.3 2.6 sort.17
  49.3 4.3 %gather_fusion.1 = bf16[64,32,768]{2,1,0:T(8,128)(2,1)} fusion(bf16[64,32,768]{2,1,0:T(8,128)(2,1)} %gather_fusion, s32[1024]{0:T(1024)S(1)} %pad_clamp_fusion), kind=kCustom, calls=%fused_computation.1 | custom fusion | bytes 6291712 | tf_op jit(solution)/shard_map/gather | solution.py:57
  58.8 128.1 %all-to-all-done = bf16[64,32,768]{2,1,0:T(8,128)(2,1)S(1)} async-done(((bf16[64,32,768]{2,1,0:T(8,128)(2,1)}), bf16[64,32,768]{2,1,0:T(8,128)(2,1)S(1)}, u32[]{:S(2)}, u32[]{:S(2)}) %all-to-all-start) | async-done | bytes 3145760 | tf_op jit(solution)/shard_map/all_to_all | solution.py:115
  186.9 2.4 gather_fusion.2
  193.0 54.2 %while.19 = (s32[]{:T(128)}, bf16[64,32,768]{2,1,0:T(8,128)(2,1)S(1)}, bf16[64,32]{1,0:T(8,128)(2,1)}, bf16[64,32,768]{2,1,0:T(8,128)(2,1)}, bf16[64,32]{1,0:T(8...) while((s32[]{:T(128)}, ...), condition=%wide.region_6.7_spmd, body=%wide.region_3.6_spmd.sunk | while | flops 38206988 | bytes 2470131 | solution.py:81
  195.8 2.1 fusion.74
  216.2 2.1 fusion.74
  222.9 2.1 fusion.74
  229.7 2.1 fusion.74
  243.3 2.1 fusion.74
  250.3 5.5 %all-to-all-start.3 = ((bf16[64,1,32]{2,1,0:T(2,128)(2,1)}), bf16[64,1,32]{2,1,0:T(2,128)(2,1)}, u32[]{:S(2)}, u32[]{:S(2)}) async-start(bf16[64,1,32]{2,1,0:T(2,128)(2,1)} %copy.33), calls=%async_computation.3 | async-start | bytes 65536 | tf_op jit(solution)/shard_map/all_to_all | solution.py:132
  255.8 2.1 broadcast.97.clone.3
  257.9 10.9 %scatter_fusion.1 = bf16[64,32,768]{2,1,0:T(8,128)(2,1)} fusion(bf16[64,32,768]{2,1,0:T(8,128)(2,1)} %broadcast.97.clone.3, s32[64]{0:T(128)S(1)} %compare_select_fusion, bf16[64,32,768]{2,1,0:T(8,128)(2,1)} %get-tuple-element.180), kind=kCustom, calls=%fused_computation.8 | custom fusion | bytes 9437440 | tf_op jit(solution)/shard_map/scatter | solution.py:82
  270.0 14.1 %all-to-all-start.2 = ((bf16[64,32,768]{2,1,0:T(8,128)(2,1)}), bf16[64,32,768]{2,1,0:T(8,128)(2,1)}, u32[]{:S(2)}, u32[]{:S(2)}) async-start(bf16[64,32,768]{2,1,0:T(8,128)(2,1)} %scatter_fusion.1), calls=%async_computation.2 | async-start | bytes 6291456 | tf_op jit(solution)/shard_map/all_to_all | solution.py:131
  291.2 2.3 collective-permute-start.3
  293.7 2.4 collective-permute-start.2
  299.0 7.1 %scatter_fusion = bf16[64,32,768]{2,1,0:T(8,128)(2,1)S(1)} fusion(bf16[64,32,768]{2,1,0:T(8,128)(2,1)S(1)} %broadcast.97.clone.2, s32[64]{0:T(128)S(1)} %compare_select_fusion, bf16[64,32,768]{2,1,0:T(8,128)(2,1)} %copy-done), kind=kCustom, calls=%fused_computation.7 | custom fusion | bytes 9437440 | tf_op jit(solution)/shard_map/scatter | solution.py:82
  309.9 111.9 %all-to-all-done.2 = bf16[64,32,768]{2,1,0:T(8,128)(2,1)} async-done(((bf16[64,32,768]{2,1,0:T(8,128)(2,1)}), bf16[64,32,768]{2,1,0:T(8,128)(2,1)}, u32[]{:S(2)}, u32[]{:S(2)}) %all-to-all-start.2) | async-done | bytes 3145760 | tf_op jit(solution)/shard_map/all_to_all | solution.py:131
  421.8 2.3 broadcast_select_fusion
  424.2 3.4 fusion.13
  (126 shorter events, 82.1 us)
Async XLA Ops:
  1.4 0.5 copy-start.5
  2.6 20.4 %copy-start.1 = (bf16[64,32]{1,0:T(8,128)(2,1)}, bf16[64,32]{1,0:T(8,128)(2,1)S(1)}, u32[]{:S(2)}) copy-start(bf16[64,32]{1,0:T(8,128)(2,1)S(1)} %gather_fusion.3) | copy-start | bytes 12292
  3.3 33.1 %all-to-all-start.1 = ((bf16[64,1,32]{2,1,0:T(2,128)(2,1)}), bf16[64,1,32]{2,1,0:T(2,128)(2,1)S(1)}, u32[]{:S(2)}, u32[]{:S(2)}) async-start(bf16[64,1,32]{2,1,0:T(2,128)(2,1)} %copy.27), calls=%async_computation.1 | async-start | bytes 65536 | tf_op jit(solution)/shard_map/all_to_all | solution.py:116
  36.3 0.6 copy-start.2
  37.0 149.9 %all-to-all-start = ((bf16[64,32,768]{2,1,0:T(8,128)(2,1)}), bf16[64,32,768]{2,1,0:T(8,128)(2,1)S(1)}, u32[]{:S(2)}, u32[]{:S(2)}) async-start(bf16[64,32,768]{2,1,0:T(8,128)(2,1)} %gather_fusion), calls=%async_computation | async-start | bytes 6291456 | tf_op jit(solution)/shard_map/all_to_all | solution.py:115
  189.3 3.6 copy-start.10
  247.2 21.6 %copy-start = (bf16[64,32,768]{2,1,0:T(8,128)(2,1)}, bf16[64,32,768]{2,1,0:T(8,128)(2,1)S(1)}, u32[]{:S(2)}) copy-start(bf16[64,32,768]{2,1,0:T(8,128)(2,1)S(1)} %get-tuple-element.179) | copy-start | bytes 9437188
  250.3 19.7 %all-to-all-start.3 = ((bf16[64,1,32]{2,1,0:T(2,128)(2,1)}), bf16[64,1,32]{2,1,0:T(2,128)(2,1)}, u32[]{:S(2)}, u32[]{:S(2)}) async-start(bf16[64,1,32]{2,1,0:T(2,128)(2,1)} %copy.33), calls=%async_computation.3 | async-start | bytes 65536 | tf_op jit(solution)/shard_map/all_to_all | solution.py:132
  268.8 17.2 %copy-start.6 = (bf16[256]{0:T(256)(128)(2,1)S(1)}, bf16[256]{0:T(256)(128)(2,1)}, u32[]{:S(2)}) copy-start(bf16[256]{0:T(256)(128)(2,1)} %copy-done.5) | copy-start | bytes 1540
  270.0 18.0 %copy-start.11 = (s32[256]{0:T(256)S(1)}, s32[256]{0:T(256)}, u32[]{:S(2)}) copy-start(s32[256]{0:T(256)} %param.6) | copy-start | bytes 3076
  270.0 151.8 %all-to-all-start.2 = ((bf16[64,32,768]{2,1,0:T(8,128)(2,1)}), bf16[64,32,768]{2,1,0:T(8,128)(2,1)}, u32[]{:S(2)}, u32[]{:S(2)}) async-start(bf16[64,32,768]{2,1,0:T(8,128)(2,1)} %scatter_fusion.1), calls=%async_computation.2 | async-start | bytes 6291456 | tf_op jit(solution)/shard_map/all_to_all | solution.py:131
  284.1 6.9 %collective-permute-start = (bf16[1,32,768]{2,1,0:T(8,128)(2,1)S(1)}, bf16[1,32,768]{2,1,0:T(8,128)(2,1)S(1)}, u32[]{:S(2)}, u32[]{:S(2)}) collective-permute-start(bf16[1,32,768]{2,1,0:T(8,128)(2,1)S(1)} %slice_bitcast_fusion), channel_id=1, source_target_pairs={{0,64},{64,128},{128,192},{192,256},{256,320},{320,384},{384,448},... | collective-permute-start | bytes 147464 | tf_op jit(solution)/shard_map/ppermute | solution.py:17
  286.1 4.8 %collective-permute-start.1 = (bf16[1,32]{1,0:T(2,128)(2,1)S(1)}, bf16[1,32]{1,0:T(2,128)(2,1)S(1)}, u32[]{:S(2)}, u32[]{:S(2)}) collective-permute-start(bf16[1,32]{1,0:T(2,128)(2,1)S(1)} %get-tuple-element.230), channel_id=1, source_target_pairs={{0,64},{64,128},{128,192},{192,256},{256,320},{320,384},{384,448},... | collective-permute-start | bytes 200 | tf_op jit(solution)/shard_map/ppermute | solution.py:17
  291.2 6.2 %collective-permute-start.3 = (bf16[1,32]{1,0:T(2,128)(2,1)S(1)}, bf16[1,32]{1,0:T(2,128)(2,1)S(1)}, u32[]{:S(2)}, u32[]{:S(2)}) collective-permute-start(bf16[1,32]{1,0:T(2,128)(2,1)S(1)} %bitcast.59), channel_id=1, source_target_pairs={{64,0},{128,64},{192,128},{256,192},{320,256},{384,320},{448,384},... | collective-permute-start | bytes 200 | tf_op jit(solution)/shard_map/ppermute | solution.py:17
  293.7 4.2 collective-permute-start.2
  309.9 114.2 %copy-start.7 = (pred[64]{0:T(512)(128)(4,1)S(1)}, pred[64]{0:T(512)(128)(4,1)}, u32[]{:S(2)}) copy-start(pred[64]{0:T(512)(128)(4,1)} %get-tuple-element.220) | copy-start | bytes 196
  424.2 3.7 copy-start.3
  424.2 3.7 copy-start.4
  424.2 3.7 copy-start.8
  424.2 3.7 copy-start.9
  424.2 3.7 copy-start.12
where the time goes:
time: 438 us; the launch traced here: 429 us
  waiting for transfers between devices  252 us (58%)
  local copies, waits for them, and re-layouts  63.3 us (14%)
  starting transfers between devices  52 us (12%)
  matrix products  46.2 us (11%)
  other arithmetic  14.2 us (3%)
    all_to_all x1, waiting for transfers between devices, local(): lax.all_to_all(my_rows, 'dev', split_axis=0, concat_axis=0, tiled=True)  128 us
    all_to_all x1, waiting for transfers between devices, local(): lax.all_to_all(far_sum, 'dev', split_axis=0, concat_axis=0, tiled=True)  112 us
    scatter x4, local copies, waits for them, and re-layouts, owned_pairs(): jnp.zeros_like(current).at[slot_order].set(current)  21.2 us
    all_to_all x1, starting transfers between devices, local(): lax.all_to_all(my_topic, 'dev', split_axis=0, concat_axis=0, tiled=True)  18.6 us
    dot_general x9, matrix products, tile_sides(): jnp.einsum('sij,sid->sjd', weights, my_rows, preferred_element_type=jnp.f...  16.8 us
    all_to_all x1, starting transfers between devices, local(): lax.all_to_all(far_sum, 'dev', split_axis=0, concat_axis=0, tiled=True)  14.1 us
    dot_general x10, matrix products, kernel_tiles(): jnp.einsum('sid,sjd->sij', left_rows, right_rows, preferred_element_type=...  13.4 us
    dynamic_slice x16, local copies, waits for them, and re-layouts, step(): lax.dynamic_slice_in_dim(member_part, first_slot, group_size, 0)  10.7 us
  transfers between devices with their start and end apart: 8, of which 5 were waited for; matrix products, arithmetic and copies ran while one was open for 12% of the time, Pallas kernels for 0%

commit v1 on v0

v1 whole, which is shorter than its diff:
```python
import functools

import jax
import jax.numpy as jnp
from jax import lax
from jax.experimental import pallas as pl
from jax.experimental.pallas import tpu as pltpu
from jax.sharding import PartitionSpec as P

BLOCK = 32
WIDE = 4
LANES = WIDE * BLOCK
PIECES = 2

SHARPNESS = 60.0
LEAKAGE = 0.3
EPSILON = 1e-06

MESH = pl.DeviceIdType.MESH


def full_hops(depth):
    return depth // 2 - 2


def counts(depth):
    hops = full_hops(depth)
    ring = 2 * hops * PIECES
    plane = depth - 1
    picked = 3 + 2 * hops * 3 + 2 * 6
    return ring + plane + picked + 3 + 4, picked


def kernel(depth, slabs, embed, topic, pairs, out, raw, own, groups, stage, tile, parts, planes, edges,
           mine, acc, weight_sum, local_sem, send_sem, recv_sem, *rings):
    hops = full_hops(depth)
    rows, width = own.shape
    blocks = rows // BLOCK
    me = lax.axis_index("dev")
    slab = lax.axis_index("topic")
    z, x = me // WIDE, lax.rem(me, WIDE)

    def node(dz, dx):
        return lax.rem(z + dz + depth, depth) * WIDE + lax.rem(x + dx + WIDE, WIDE)

    def neighbour(by):
        return lax.rem(slab + by + slabs, slabs)

    load = pltpu.make_async_copy(embed, raw, local_sem)
    load.start()

    barrier = pltpu.get_barrier_semaphore()
    takers = [(0, o) for o in (1, 2, 3)]
    takers += [(s, o) for s in (1, -1) for o in range(WIDE)]
    takers += [(2, 0), (2, 1), (-2, 2), (-2, 3)]
    for dz, dx in takers:
        pl.semaphore_signal(barrier, inc=1, device_id={"dev": node(-dz, -dx)}, device_id_type=MESH)
    for by in (1, -1):
        pl.semaphore_signal(barrier, inc=1, device_id={"topic": neighbour(by)}, device_id_type=MESH)

    started = []
    used = [0, 0]

    def copy(src, dst, **device):
        k = used[0]
        used[0] += 1
        c = pltpu.make_async_remote_copy(
            src_ref=src, dst_ref=dst, send_sem=send_sem.at[k], recv_sem=recv_sem.at[k],
            device_id=device, device_id_type=MESH)
        c.start()
        started.append(c)
        return c

    ids = topic[...].astype(jnp.float32)
    lane = lax.broadcasted_iota(jnp.int32, (1, LANES), 1)
    lane_part = lane // BLOCK
    of_block = lax.broadcasted_iota(jnp.int32, (blocks, rows), 0) == lax.broadcasted_iota(
        jnp.int32, (blocks, rows), 1) // BLOCK
    same_place = lax.rem(lax.broadcasted_iota(jnp.int32, (rows, LANES), 0), BLOCK) == lax.rem(
        lax.broadcasted_iota(jnp.int32, (rows, LANES), 1), BLOCK)
    tile[...] = jnp.dot(
        jnp.where(of_block, ids, 0.0).astype(jnp.bfloat16), same_place.astype(jnp.bfloat16),
        preferred_element_type=jnp.float32)
    diagonal = lax.broadcasted_iota(jnp.int32, (rows, rows), 0) == lax.broadcasted_iota(
        jnp.int32, (rows, rows), 1)
    mine[...] = jnp.dot(
        jnp.where(diagonal, ids, 0.0).astype(jnp.bfloat16), jnp.ones((rows, LANES), jnp.bfloat16),
        preferred_element_type=jnp.float32)

    load.wait()
    values = raw[...].astype(jnp.float32)
    scale = lax.rsqrt(jnp.mean(values * values, axis=-1, keepdims=True) + EPSILON)
    own[...] = (values * scale).astype(jnp.bfloat16)

    pl.semaphore_wait(barrier, len(takers) + 2)

    def ring_step(way, hop, piece):
        src = own if hop == 1 else rings[way * hops + hop - 2]
        part = pl.ds(piece * (rows // PIECES), rows // PIECES)
        return copy(src.at[part], rings[way * hops + hop - 1].at[part], dev=node(1 - 2 * way, 0))

    def pick(src, owner, takers):
        count = len(takers)
        at = lax.broadcasted_iota(jnp.int32, (count * BLOCK, rows), 0)
        wanted = jnp.full((count * BLOCK, rows), pairs[0, owner, takers[0]], jnp.int32)
        for i in range(1, count):
            wanted = jnp.where(at >= i * BLOCK, pairs[0, owner, takers[i]], wanted)
        source = jnp.maximum(wanted, 0) * BLOCK + lax.rem(at, BLOCK)
        choice = lax.broadcasted_iota(jnp.int32, (count * BLOCK, rows), 1) == source
        return jnp.dot(
            choice.astype(jnp.bfloat16), src[...], preferred_element_type=jnp.float32
        ).astype(jnp.bfloat16)

    def slot(step, way):
        return groups.at[pl.ds(pl.multiple_of(step * rows + way * LANES + x * BLOCK, BLOCK), BLOCK)]

    def picks(src, step, way, dz_owner, dz_taker, offsets):
        takers = [node(dz_taker, o) for o in offsets]
        picked = pick(src, node(dz_owner, 0), takers)
        copies = []
        for i, (o, taker) in enumerate(zip(offsets, takers)):
            block = picked[i * BLOCK:(i + 1) * BLOCK]
            if dz_taker == 0 and o == 0:
                slot(step, way)[...] = block
                continue
            spot = stage.at[pl.ds(used[1] * BLOCK, BLOCK)]
            used[1] += 1
            spot[...] = block
            copies.append(copy(spot, slot(step, way), dev=taker))
        return copies

    in_ring = {}
    for piece in range(PIECES):
        for way in (0, 1):
            in_ring[way, 1, piece] = ring_step(way, 1, piece)

    beside = [copy(tile, parts.at[x], dev=node(0, o)) for o in (1, 2, 3)]
    in_slots = {0: picks(own, 0, 0, 0, 0, range(WIDE))}
    border = [
        copy(tile, edges.at[0], topic=neighbour(1)),
        copy(tile, edges.at[1], topic=neighbour(-1)),
        copy(own.at[pl.ds(rows - BLOCK, BLOCK)], groups.at[pl.ds(LANES, BLOCK)], topic=neighbour(1)),
        copy(own.at[pl.ds(0, BLOCK)], groups.at[pl.ds(LANES + BLOCK, BLOCK)], topic=neighbour(-1)),
    ]
    parts[x] = tile[...]
    groups[pl.ds(LANES + 2 * BLOCK, 2 * BLOCK), :] = jnp.zeros((2 * BLOCK, width), jnp.bfloat16)

    row_block = lax.broadcasted_iota(jnp.int32, (rows, LANES), 0) // BLOCK

    def weigh(scores, topics, keep):
        factor = jnp.where(mine[...] == topics, 1.0, LEAKAGE)
        w = jnp.exp(scores * (SHARPNESS / width)) * factor
        return jnp.where(keep, w, 0.0).astype(jnp.bfloat16)

    def against(theirs, halves, first=False):
        scores = lax.dot_general(
            own[...], theirs, (((1,), (1,)), ((), ())), preferred_element_type=jnp.float32)
        ws = [
            weigh(scores[:, i * LANES:(i + 1) * LANES], topics, keep)
            for i, (topics, keep) in enumerate(halves)
        ]
        totals = sum(w.astype(jnp.float32) for w in ws)
        w = jnp.concatenate(ws, 1) if len(ws) > 1 else ws[0]
        sums = jnp.dot(w, theirs, preferred_element_type=jnp.float32)
        if first:
            acc[...] = sums
            weight_sum[...] = totals
        else:
            acc[...] += sums
            weight_sum[...] += totals

    def by_part(values):
        row = jnp.where(lane_part == 0, values[0], values[1])
        for j in (2, 3):
            row = jnp.where(lane_part == j, values[j], row)
        return row

    def plane_half(dz, plane):
        owners = [lax.rem(z + dz + depth, depth) * WIDE + j for j in range(WIDE)]
        theirs = by_part([pairs[0, n, me] for n in owners])
        ours = by_part([pairs[0, me, n] for n in owners])
        at = lax.broadcasted_iota(jnp.int32, (blocks, LANES), 0)
        topics = jnp.sum(jnp.where(at == theirs, planes[plane], 0.0), axis=0, keepdims=True)
        return topics, row_block == ours

    own_halves = []
    row_at = lax.broadcasted_iota(jnp.int32, (rows, LANES), 0)
    lane_at = lax.broadcasted_iota(jnp.int32, (rows, LANES), 1)
    for i in range(rows // LANES):
        topics = tile[pl.ds(i * WIDE, 1), :]
        for j in range(1, WIDE):
            topics = jnp.where(lane_part == j, tile[pl.ds(i * WIDE + j, 1), :], topics)
        own_halves.append((topics, row_at != lane_at + i * LANES))
    against(own[...], own_halves, first=True)

    for c in beside:
        c.wait_recv()
    plane = parts[0]
    for j in range(1, WIDE):
        plane = jnp.where(lane_part == j, parts[j], plane)
    planes[0] = plane

    far = depth // 2

    def plane_at(way, hop):
        return 0 if hop == 0 else 2 * hop - 1 + way

    in_plane = {}

    def pass_plane(hop):
        for way in (0, 1):
            if hop and (way, hop) in in_plane:
                in_plane[way, hop].wait_recv()
            if hop + 1 < far or (hop + 1 == far and way == 0):
                in_plane[way, hop + 1] = copy(
                    planes.at[plane_at(way, hop)], planes.at[plane_at(way, hop + 1)],
                    dev=node(1 - 2 * way, 0))

    def finish(step):
        for c in in_slots[step]:
            c.wait_recv()
        if step == 0:
            for c in border:
                c.wait_recv()
            topics = jnp.where(lane_part == 0, edges[0, pl.ds(blocks - 1, 1), :], edges[1, pl.ds(0, 1), :])
            before = jnp.where(slab > 0, 0, -1)
            behind = jnp.where(slab < slabs - 1, blocks - 1, -1)
            ours = jnp.where(lane_part == 0, before, jnp.where(lane_part == 1, behind, -1))
            halves = [plane_half(0, 0), (topics, row_block == ours)]
        elif step == far:
            halves = [plane_half(-far, plane_at(0, far))]
        else:
            halves = [plane_half(-step, plane_at(0, step)), plane_half(step, plane_at(1, step))]
        against(groups[pl.ds(step * rows, LANES * len(halves)), :], halves)

    pass_plane(0)
    for hop in range(1, hops + 1):
        for piece in range(PIECES):
            for way in (0, 1):
                in_ring[way, hop, piece].wait_recv()
                if hop < hops:
                    in_ring[way, hop + 1, piece] = ring_step(way, hop + 1, piece)
        in_slots[hop] = []
        if hop == hops:
            in_slots[far - 1] = []
            in_slots[far] = []
            for way, offsets in ((0, (0, 1)), (1, (2, 3))):
                ring, by = rings[way * hops + hop - 1], 1 - 2 * way
                in_slots[far] += picks(ring, far, 0, -by * hop, by * 2, offsets)
                in_slots[far - 1] += picks(ring, far - 1, way, -by * hop, by, range(WIDE))
        for way in (0, 1):
            ring, by = rings[way * hops + hop - 1], 1 - 2 * way
            in_slots[hop] += picks(ring, hop, way, -by * hop, 0, range(WIDE))
        pass_plane(hop)
        finish(hop - 1)
    pass_plane(far - 1)
    finish(hops)
    pass_plane(far)
    finish(far - 1)
    finish(far)

    total = jnp.sum(weight_sum[...], axis=1, keepdims=True)
    out[...] = (acc[...] / total).astype(out.dtype)
    for c in started:
        c.wait_send()


def local(depth, slabs, embeddings, topic_ids, pair_blocks):
    rows, width = embeddings.shape
    hops = full_hops(depth)
    blocks = rows // BLOCK
    copies, picked = counts(depth)
    whole = pltpu.VMEM((rows, width), jnp.bfloat16)
    ids = pltpu.VMEM((blocks, LANES), jnp.float32)
    return pl.pallas_call(
        functools.partial(kernel, depth, slabs),
        out_shape=jax.ShapeDtypeStruct((rows, width), jnp.bfloat16),
        in_specs=[
            pl.BlockSpec(memory_space=pl.ANY),
            pl.BlockSpec(memory_space=pltpu.VMEM),
            pl.BlockSpec(memory_space=pltpu.SMEM),
        ],
        out_specs=pl.BlockSpec(memory_space=pltpu.VMEM),
        scratch_shapes=[
            whole,
            whole,
            pltpu.VMEM(((depth // 2) * rows + LANES, width), jnp.bfloat16),
            pltpu.VMEM((picked * BLOCK, width), jnp.bfloat16),
            ids,
            pltpu.VMEM((WIDE, blocks, LANES), jnp.float32),
            pltpu.VMEM((depth, blocks, LANES), jnp.float32),
            pltpu.VMEM((2, blocks, LANES), jnp.float32),
            pltpu.VMEM((rows, LANES), jnp.float32),
            pltpu.VMEM((rows, width), jnp.float32),
            pltpu.VMEM((rows, LANES), jnp.float32),
            pltpu.SemaphoreType.DMA,
            pltpu.SemaphoreType.DMA((copies,)),
            pltpu.SemaphoreType.DMA((copies,)),
        ] + [whole] * (2 * hops),
        compiler_params=pltpu.CompilerParams(
            collective_id=0, has_side_effects=True, vmem_limit_bytes=40 * 2**20),
    )(embeddings, topic_ids.reshape(1, rows), pair_blocks)


def solution(mesh):
    return jax.shard_map(
        functools.partial(local, mesh.shape["dev"] // WIDE, mesh.shape["topic"]),
        mesh=mesh,
        in_specs=(P(("topic", "dev"), None), P(("topic", "dev")), P("topic", None, None)),
        out_specs=P(("topic", "dev"), None),
        check_vma=False,
    )
```

time: 438 us -> 87.1 us (0.20); the launches traced: 429 us -> 86.5 us
  waiting for transfers between devices: 252 us -> 0 us
  Pallas kernels: 0 us -> 83.3 us
  local copies, waits for them, and re-layouts: 63.3 us -> 3.18 us
  starting transfers between devices: 52 us -> 0 us
  matrix products: 46.2 us -> 0 us
  other arithmetic: 14.2 us -> 0 us
    all_to_all x4 -> x0, waiting for transfers between devices: 251 us -> none  [the longest x1 128 us: local(): lax.all_to_all(my_rows, 'dev', split_axis=0, concat_axis=0, tiled=True)]
    pallas_call x0 -> x1, Pallas kernels: none -> 83.3 us  [local(): pl.pallas_call(functools.partial(kernel, depth, slabs), out_shape=jax.Sha...]
    dot_general x31 -> x0, matrix products: 46.2 us -> none  [the longest x9 16.8 us: tile_sides(): jnp.einsum('sij,sid->sjd', weights, my_rows, preferred_element_type=jnp.f...]
    all_to_all x4 -> x0, starting transfers between devices: 43.4 us -> none  [the longest x1 18.6 us: local(): lax.all_to_all(my_topic, 'dev', split_axis=0, concat_axis=0, tiled=True)]
    scatter x4 -> x0, local copies, waits for them, and re-layouts: 21.2 us -> none  [owned_pairs(): jnp.zeros_like(current).at[slot_order].set(current)]
    gather x7 -> x0, local copies, waits for them, and re-layouts: 15 us -> none  [the longest x1 4.3 us: owned_pairs(): my_rows[slot_order]]
    dynamic_slice x16 -> x0, local copies, waits for them, and re-layouts: 10.7 us -> none  [step(): lax.dynamic_slice_in_dim(member_part, first_slot, group_size, 0)]
    ppermute x4 -> x0, starting transfers between devices: 8.53 us -> none  [from_behind(): return lax.ppermute(array, axis, pairs)]
  transfers between devices with their start and end apart: 8 -> 0, of which waited for: 5 -> 0; matrix products, arithmetic and copies ran while one was open for 12% -> 0% of each run, Pallas kernels for 0% -> 0%
where the time goes in v1:
time: 87.1 us; the launch traced here: 86.5 us
  Pallas kernels  83.3 us (96%)
  local copies, waits for them, and re-layouts  3.18 us (4%)
    pallas_call x1, Pallas kernels, local(): pl.pallas_call(functools.partial(kernel, depth, slabs), out_shape=jax.Sha...  83.3 us
    unnamed x7, local copies, waits for them, and re-layouts  3.18 us

profile of v1, /device:TPU:24, one launch (start us, length us, event | category | flops | bytes accessed | tf_op | source)
XLA Modules:
  0.0 86.5 jit_solution(3580310558496424586)
XLA Ops:
  0.0 0.0 copy-start.2
  0.0 0.7 copy-done.2
  0.7 0.0 copy-start
  0.7 1.0 %copy-done = bf16[256,768]{1,0:T(8,128)(2,1)S(1)} copy-done((bf16[256,768]{1,0:T(8,128)(2,1)S(1)}, bf16[256,768]{1,0:T(8,128)(2,1)}, u32[]{:S(2)}) %copy-start) | copy-done | bytes 393240
  1.7 0.0 copy-start.1
  1.7 0.8 copy-done.1
  2.4 83.3 %shard_map.37 = bf16[256,768]{1,0:T(8,128)(2,1)S(1)} custom-call(bf16[256,768]{1,0:T(8,128)(2,1)S(1)} %copy-done, s32[1,256]{1,0:T(1,128)S(1)} %bitcast.1, s32[1,64,64]{2,1,0:T(8,128)S(1)} %copy-done.1), custom_call_target="tpu_custom_call" | custom-call | tf_op jit(solution)/shard_map/pallas_call | solution.py:275
  85.7 0.7 copy.5
Async XLA Ops:
  0.0 0.7 copy-start.2
  0.7 1.0 %copy-start = (bf16[256,768]{1,0:T(8,128)(2,1)S(1)}, bf16[256,768]{1,0:T(8,128)(2,1)}, u32[]{:S(2)}) copy-start(bf16[256,768]{1,0:T(8,128)(2,1)} %embed.1) | copy-start | bytes 1179652
  1.7 0.8 copy-start.1

commit v2 on v1

v2 whole, which is shorter than its diff:
```python
import functools

import jax
import jax.numpy as jnp
from jax import lax
from jax.experimental import pallas as pl
from jax.experimental.pallas import tpu as pltpu
from jax.sharding import PartitionSpec as P

BLOCK = 32
WIDE = 4
LANES = WIDE * BLOCK
PIECES = 2

SHARPNESS = 60.0
LEAKAGE = 0.3
EPSILON = 1e-06

MESH = pl.DeviceIdType.MESH


def full_hops(depth):
    return depth // 2 - 2


def picked_blocks(depth):
    return 3 + 2 * full_hops(depth) * 3 + 2 * 6


def kernel(depth, slabs, embed, topic, pairs, out, raw, topic_row, pair, own, groups, stage, tile, parts,
           planes, edges, mine, ours_at, theirs_at, acc, weight_sum, local_sem, send_sem, ring_sem,
           plane_sem, slot_sem, tile_sem, *rings):
    hops = full_hops(depth)
    rows, width = own.shape
    blocks = rows // BLOCK
    members = depth * WIDE
    far = depth // 2
    me = lax.axis_index("dev")
    slab = lax.axis_index("topic")
    z, x = me // WIDE, lax.rem(me, WIDE)

    def node(dz, dx):
        return lax.rem(z + dz + depth, depth) * WIDE + lax.rem(x + dx + WIDE, WIDE)

    def neighbour(by):
        return lax.rem(slab + by + slabs, slabs)

    loads = [
        pltpu.make_async_copy(src, dst, local_sem.at[i])
        for i, (src, dst) in enumerate(((embed, raw), (topic, topic_row), (pairs, pair)))
    ]
    for c in loads:
        c.start()

    barrier = pltpu.get_barrier_semaphore()
    takers = [(0, o) for o in (1, 2, 3)]
    takers += [(s, o) for s in (1, -1) for o in range(WIDE)]
    takers += [(2, 0), (2, 1), (-2, 2), (-2, 3)]
    for dz, dx in takers:
        pl.semaphore_signal(barrier, inc=1, device_id={"dev": node(-dz, -dx)}, device_id_type=MESH)
    for by in (1, -1):
        pl.semaphore_signal(barrier, inc=1, device_id={"topic": neighbour(by)}, device_id_type=MESH)

    RING, BLOCKS, EDGES, TILES = (0, 1), 2, 3, 4
    tiles_sent = [0]

    def copy(kind, arrived, src, dst, **device):
        c = pltpu.make_async_remote_copy(
            src_ref=src, dst_ref=dst, send_sem=send_sem.at[kind], recv_sem=arrived,
            device_id=device, device_id_type=MESH)
        c.start()
        if kind == TILES:
            tiles_sent[0] += 1
        return c

    def await_bytes(sem, like):
        pltpu.make_async_copy(like, like, sem).wait()

    loads[0].wait()
    values = raw[...].astype(jnp.float32)
    scale = lax.rsqrt(jnp.mean(values * values, axis=-1, keepdims=True) + EPSILON)
    own[...] = (values * scale).astype(jnp.bfloat16)

    pl.semaphore_wait(barrier, len(takers) + 2)

    def ring_step(way, hop, piece):
        src = own if hop == 1 else rings[way * hops + hop - 2]
        part = pl.ds(piece * (rows // PIECES), rows // PIECES)
        return copy(
            RING[way], ring_sem.at[way, hop - 1, piece], src.at[part],
            rings[way * hops + hop - 1].at[part], dev=node(1 - 2 * way, 0))

    in_ring = {}
    for piece in range(PIECES):
        for way in (0, 1):
            in_ring[way, 1, piece] = ring_step(way, 1, piece)

    loads[1].wait()
    ids = topic_row[...].astype(jnp.float32)
    lane_part = lax.broadcasted_iota(jnp.int32, (1, LANES), 1) // BLOCK
    of_block = lax.broadcasted_iota(jnp.int32, (blocks, rows), 0) == lax.broadcasted_iota(
        jnp.int32, (blocks, rows), 1) // BLOCK
    same_place = lax.rem(lax.broadcasted_iota(jnp.int32, (rows, LANES), 0), BLOCK) == lax.rem(
        lax.broadcasted_iota(jnp.int32, (rows, LANES), 1), BLOCK)
    tile[...] = jnp.dot(
        jnp.where(of_block, ids, 0.0).astype(jnp.bfloat16), same_place.astype(jnp.bfloat16),
        preferred_element_type=jnp.float32)
    for o in (1, 2, 3):
        copy(TILES, tile_sem, tile, parts.at[x], dev=node(0, o))
    copy(TILES, slot_sem.at[far + 1], tile, edges.at[0], topic=neighbour(1))
    copy(TILES, slot_sem.at[far + 1], tile, edges.at[1], topic=neighbour(-1))
    parts[x] = tile[...]
    copy(EDGES, slot_sem.at[0], own.at[pl.ds(rows - BLOCK, BLOCK)],
         groups.at[pl.ds(LANES, BLOCK)], topic=neighbour(1))
    copy(EDGES, slot_sem.at[0], own.at[pl.ds(0, BLOCK)],
         groups.at[pl.ds(LANES + BLOCK, BLOCK)], topic=neighbour(-1))

    def choose(owner, takers):
        count = len(takers) * BLOCK
        at = lax.broadcasted_iota(jnp.int32, (count, 1), 0)
        taker = jnp.full((count, 1), takers[0], jnp.int32)
        for i in range(1, len(takers)):
            taker = jnp.where(at >= i * BLOCK, takers[i], taker)
        named = jnp.where(
            lax.broadcasted_iota(jnp.int32, (count, members), 1) == taker,
            pair[0, pl.ds(owner, 1), :].astype(jnp.float32), 0.0)
        block = jnp.maximum(jnp.sum(named, axis=1, keepdims=True), 0.0).astype(jnp.int32)
        source = block * BLOCK + lax.rem(at, BLOCK)
        return (lax.broadcasted_iota(jnp.int32, (count, rows), 1) == source).astype(jnp.bfloat16)

    def slot(step, way):
        return groups.at[pl.ds(pl.multiple_of(step * rows + way * LANES + x * BLOCK, BLOCK), BLOCK)]

    staged = [0]

    def picks(dz_owner, dz_taker, offsets):
        takers = [node(dz_taker, o) for o in offsets]
        choice = choose(node(dz_owner, 0), takers)

        def send(src, step, way):
            picked = jnp.dot(choice, src[...], preferred_element_type=jnp.float32).astype(jnp.bfloat16)
            for i, (o, taker) in enumerate(zip(offsets, takers)):
                block = picked[i * BLOCK:(i + 1) * BLOCK]
                if dz_taker == 0 and o == 0:
                    slot(step, way)[...] = block
                    continue
                spot = stage.at[pl.ds(staged[0] * BLOCK, BLOCK)]
                staged[0] += 1
                spot[...] = block
                copy(BLOCKS, slot_sem.at[step], spot, slot(step, way), dev=taker)

        return send

    loads[2].wait()
    picks(0, 0, range(WIDE))(own, 0, 0)
    groups[pl.ds(LANES + 2 * BLOCK, 2 * BLOCK), :] = jnp.zeros((2 * BLOCK, width), jnp.bfloat16)

    ones = jnp.ones((rows, LANES), jnp.bfloat16)
    diagonal = lax.broadcasted_iota(jnp.int32, (rows, rows), 0) == lax.broadcasted_iota(
        jnp.int32, (rows, rows), 1)
    mine[...] = jnp.dot(
        jnp.where(diagonal, ids, 0.0).astype(jnp.bfloat16), ones, preferred_element_type=jnp.float32)

    in_plane_of = lax.broadcasted_iota(jnp.int32, (depth, members), 0) == lax.broadcasted_iota(
        jnp.int32, (depth, members), 1) // WIDE
    spread = lax.rem(lax.broadcasted_iota(jnp.int32, (members, LANES), 0), WIDE) == lax.broadcasted_iota(
        jnp.int32, (members, LANES), 1) // BLOCK
    my_row = pair[0, pl.ds(me, 1), :].astype(jnp.float32)
    ours_at[...] = jnp.dot(
        jnp.where(in_plane_of, my_row, 0.0).astype(jnp.bfloat16), spread.astype(jnp.bfloat16),
        preferred_element_type=jnp.float32)
    my_column = jnp.sum(
        jnp.where(lax.broadcasted_iota(jnp.int32, (members, members), 1) == me,
                  pair[0].astype(jnp.float32), 0.0), axis=1, keepdims=True)
    theirs_at[...] = jnp.dot(
        in_plane_of.astype(jnp.bfloat16), jnp.where(spread, my_column, 0.0).astype(jnp.bfloat16),
        preferred_element_type=jnp.float32)

    row_block = (lax.broadcasted_iota(jnp.int32, (rows, LANES), 0) // BLOCK).astype(jnp.float32)
    block_at = lax.broadcasted_iota(jnp.int32, (blocks, LANES), 0).astype(jnp.float32)

    def weigh(scores, topics, keep):
        factor = jnp.where(mine[...] == topics, 1.0, LEAKAGE)
        w = jnp.exp(scores * (SHARPNESS / width)) * factor
        return jnp.where(keep, w, 0.0).astype(jnp.bfloat16)

    def against(theirs, halves, first=False):
        scores = lax.dot_general(
            own[...], theirs, (((1,), (1,)), ((), ())), preferred_element_type=jnp.float32)
        ws = [
            weigh(scores[:, i * LANES:(i + 1) * LANES], topics, keep)
            for i, (topics, keep) in enumerate(halves)
        ]
        totals = sum(w.astype(jnp.float32) for w in ws)
        w = jnp.concatenate(ws, 1) if len(ws) > 1 else ws[0]
        sums = jnp.dot(w, theirs, preferred_element_type=jnp.float32)
        if first:
            acc[...] = sums
            weight_sum[...] = totals
        else:
            acc[...] += sums
            weight_sum[...] += totals

    def plane_half(dz, plane):
        at = lax.rem(z + dz + depth, depth)
        theirs, ours = theirs_at[pl.ds(at, 1), :], ours_at[pl.ds(at, 1), :]
        topics = jnp.sum(jnp.where(block_at == theirs, planes[plane], 0.0), axis=0, keepdims=True)
        return topics, row_block == ours

    own_halves = []
    row_at = lax.broadcasted_iota(jnp.int32, (rows, LANES), 0)
    lane_at = lax.broadcasted_iota(jnp.int32, (rows, LANES), 1)
    for i in range(rows // LANES):
        topics = tile[pl.ds(i * WIDE, 1), :]
        for j in range(1, WIDE):
            topics = jnp.where(lane_part == j, tile[pl.ds(i * WIDE + j, 1), :], topics)
        own_halves.append((topics, row_at != lane_at + i * LANES))
    against(own[...], own_halves, first=True)

    await_bytes(tile_sem, parts.at[pl.ds(0, WIDE - 1)])
    plane = parts[0]
    for j in range(1, WIDE):
        plane = jnp.where(lane_part == j, parts[j], plane)
    planes[0] = plane

    def plane_at(way, hop):
        return 0 if hop == 0 else 2 * hop - 1 + way

    in_plane = {}

    def pass_plane(hop):
        for way in (0, 1):
            if hop and (way, hop) in in_plane:
                in_plane[way, hop].wait_recv()
            if hop + 1 < far or (hop + 1 == far and way == 0):
                in_plane[way, hop + 1] = copy(
                    TILES, plane_sem.at[way, hop], planes.at[plane_at(way, hop)], planes.at[plane_at(way, hop + 1)],
                    dev=node(1 - 2 * way, 0))

    def finish(step):
        blocks_in = {0: WIDE - 1 + 2, far - 1: 2 * WIDE, far: WIDE}.get(step, 2 * (WIDE - 1))
        await_bytes(slot_sem.at[step], groups.at[pl.ds(step * rows, blocks_in * BLOCK)])
        if step == 0:
            await_bytes(slot_sem.at[far + 1], edges)
            topics = jnp.where(lane_part == 0, edges[0, pl.ds(blocks - 1, 1), :], edges[1, pl.ds(0, 1), :])
            before = jnp.where(slab > 0, 0.0, -1.0)
            behind = jnp.where(slab < slabs - 1, blocks - 1.0, -1.0)
            ours = jnp.where(lane_part == 0, before, jnp.where(lane_part == 1, behind, -1.0))
            halves = [plane_half(0, 0), (topics, row_block == ours)]
        elif step == far:
            halves = [plane_half(-far, plane_at(0, far))]
        else:
            halves = [plane_half(-step, plane_at(0, step)), plane_half(step, plane_at(1, step))]
        against(groups[pl.ds(step * rows, LANES * len(halves)), :], halves)

    pass_plane(0)
    for hop in range(1, hops + 1):
        sends = []
        for way, offsets in ((0, (0, 1)), (1, (2, 3))):
            ring, by = rings[way * hops + hop - 1], 1 - 2 * way
            if hop == hops:
                sends.append((picks(-by * hop, by * 2, offsets), ring, far, 0))
                sends.append((picks(-by * hop, by, range(WIDE)), ring, far - 1, way))
        for way in (0, 1):
            ring, by = rings[way * hops + hop - 1], 1 - 2 * way
            sends.append((picks(-by * hop, 0, range(WIDE)), ring, hop, way))
        for piece in range(PIECES):
            for way in (0, 1):
                in_ring[way, hop, piece].wait_recv()
                if hop < hops:
                    in_ring[way, hop + 1, piece] = ring_step(way, hop + 1, piece)
        for send, ring, step, way in sends:
            send(ring, step, way)
        pass_plane(hop)
        finish(hop - 1)
    pass_plane(far - 1)
    finish(hops)
    pass_plane(far)
    finish(far)
    finish(far - 1)

    total = jnp.sum(weight_sum[...], axis=1, keepdims=True)
    out[...] = (acc[...] / total).astype(out.dtype)
    for way in (0, 1):
        await_bytes(send_sem.at[RING[way]], groups.at[pl.ds(0, hops * rows)])
    await_bytes(send_sem.at[BLOCKS], stage)
    await_bytes(send_sem.at[EDGES], groups.at[pl.ds(0, 2 * BLOCK)])
    await_bytes(send_sem.at[TILES], mine.at[pl.ds(0, tiles_sent[0] * blocks)])


def local(depth, slabs, embeddings, topic_ids, pair_blocks):
    rows, width = embeddings.shape
    hops = full_hops(depth)
    blocks = rows // BLOCK
    far = depth // 2
    whole = pltpu.VMEM((rows, width), jnp.bfloat16)
    ids = pltpu.VMEM((blocks, LANES), jnp.float32)
    return pl.pallas_call(
        functools.partial(kernel, depth, slabs),
        out_shape=jax.ShapeDtypeStruct((rows, width), jnp.bfloat16),
        in_specs=[pl.BlockSpec(memory_space=pl.ANY)] * 3,
        out_specs=pl.BlockSpec(memory_space=pltpu.VMEM),
        scratch_shapes=[
            whole,
            pltpu.VMEM((1, rows), jnp.int32),
            pltpu.VMEM(pair_blocks.shape, jnp.int32),
            whole,
            pltpu.VMEM((far * rows + LANES, width), jnp.bfloat16),
            pltpu.VMEM((picked_blocks(depth) * BLOCK, width), jnp.bfloat16),
            ids,
            pltpu.VMEM((WIDE, blocks, LANES), jnp.float32),
            pltpu.VMEM((depth, blocks, LANES), jnp.float32),
            pltpu.VMEM((2, blocks, LANES), jnp.float32),
            pltpu.VMEM((rows, LANES), jnp.float32),
            pltpu.VMEM((depth, LANES), jnp.float32),
            pltpu.VMEM((depth, LANES), jnp.float32),
            pltpu.VMEM((rows, width), jnp.float32),
            pltpu.VMEM((rows, LANES), jnp.float32),
            pltpu.SemaphoreType.DMA((3,)),
            pltpu.SemaphoreType.DMA((5,)),
            pltpu.SemaphoreType.DMA((2, hops, PIECES)),
            pltpu.SemaphoreType.DMA((2, far)),
            pltpu.SemaphoreType.DMA((far + 2,)),
            pltpu.SemaphoreType.DMA,
        ] + [whole] * (2 * hops),
        compiler_params=pltpu.CompilerParams(
            collective_id=0, has_side_effects=True, vmem_limit_bytes=60 * 2**20),
    )(embeddings, topic_ids.reshape(1, rows), pair_blocks)


def solution(mesh):
    return jax.shard_map(
        functools.partial(local, mesh.shape["dev"] // WIDE, mesh.shape["topic"]),
        mesh=mesh,
        in_specs=(P(("topic", "dev"), None), P(("topic", "dev")), P("topic", None, None)),
        out_specs=P(("topic", "dev"), None),
        check_vma=False,
    )
```

time: 87.1 us -> 83.7 us (0.961)
  Pallas kernels: 83.3 us -> 81.4 us
  local copies, waits for them, and re-layouts: 3.18 us -> 1.77 us
    pallas_call x1, Pallas kernels: 83.3 us -> 81.4 us  [local(): pl.pallas_call(functools.partial(kernel, depth, slabs), out_shape=jax.Sha...]
    unnamed x7 -> x1, local copies, waits for them, and re-layouts: 3.18 us -> 1.77 us
where the time goes in v2:
time: 83.7 us; the launch traced here: 83.2 us
  Pallas kernels  81.4 us (97%)
  local copies, waits for them, and re-layouts  1.77 us (2%)
    pallas_call x1, Pallas kernels, local(): pl.pallas_call(functools.partial(kernel, depth, slabs), out_shape=jax.Sha...  81.4 us
    unnamed x1, local copies, waits for them, and re-layouts  1.77 us

profile of v2, /device:TPU:24, one launch (start us, length us, event | category | flops | bytes accessed | tf_op | source)
XLA Modules:
  0.0 83.2 jit_solution(16209992419818600221)
XLA Ops:
  0.0 81.4 %shard_map.37 = bf16[256,768]{1,0:T(8,128)(2,1)} custom-call(bf16[256,768]{1,0:T(8,128)(2,1)} %embed.1, s32[1,256]{1,0:T(1,128)} %bitcast.1, s32[1,64,64]{2,1,0:T(8,128)} %pairs.1), custom_call_target="tpu_custom_call" | custom-call | tf_op jit(solution)/shard_map/pallas_call | solution.py:298
  81.4 1.8 %copy.5 = bf16[256,768]{1,0:T(8,128)(2,1)} copy(bf16[256,768]{1,0:T(8,128)(2,1)} %shard_map.37) | data formatting | bytes 786432

commit v3 on v2

--- a/solution.py
+++ b/solution.py
@@ -83,12 +83,14 @@
 
     pl.semaphore_wait(barrier, len(takers) + 2)
 
+    def part(piece):
+        return pl.ds(piece * (width // PIECES), width // PIECES)
+
     def ring_step(way, hop, piece):
         src = own if hop == 1 else rings[way * hops + hop - 2]
-        part = pl.ds(piece * (rows // PIECES), rows // PIECES)
         return copy(
-            RING[way], ring_sem.at[way, hop - 1, piece], src.at[part],
-            rings[way * hops + hop - 1].at[part], dev=node(1 - 2 * way, 0))
+            RING[way], ring_sem.at[way, hop - 1, piece], src.at[:, part(piece)],
+            rings[way * hops + hop - 1].at[:, part(piece)], dev=node(1 - 2 * way, 0))
 
     in_ring = {}
     for piece in range(PIECES):
@@ -137,22 +139,31 @@
         takers = [node(dz_taker, o) for o in offsets]
         choice = choose(node(dz_owner, 0), takers)
 
-        def send(src, step, way):
-            picked = jnp.dot(choice, src[...], preferred_element_type=jnp.float32).astype(jnp.bfloat16)
-            for i, (o, taker) in enumerate(zip(offsets, takers)):
+        spots = []
+        for o in offsets:
+            local = dz_taker == 0 and o == 0
+            spots.append(None if local else stage.at[pl.ds(staged[0] * BLOCK, BLOCK)])
+            staged[0] += not local
+
+        def send(src, step, way, piece):
+            picked = jnp.dot(
+                choice, src[:, part(piece)], preferred_element_type=jnp.float32).astype(jnp.bfloat16)
+            for i, (taker, spot) in enumerate(zip(takers, spots)):
                 block = picked[i * BLOCK:(i + 1) * BLOCK]
-                if dz_taker == 0 and o == 0:
-                    slot(step, way)[...] = block
+                there = slot(step, way).at[:, part(piece)]
+                if spot is None:
+                    there[...] = block
                     continue
-                spot = stage.at[pl.ds(staged[0] * BLOCK, BLOCK)]
-                staged[0] += 1
-                spot[...] = block
-                copy(BLOCKS, slot_sem.at[step], spot, slot(step, way), dev=taker)
+                here = spot.at[:, part(piece)]
+                here[...] = block
+                copy(BLOCKS, slot_sem.at[step], here, there, dev=taker)
 
         return send
 
     loads[2].wait()
-    picks(0, 0, range(WIDE))(own, 0, 0)
+    pick_own = picks(0, 0, range(WIDE))
+    for piece in range(PIECES):
+        pick_own(own, 0, 0, piece)
     groups[pl.ds(LANES + 2 * BLOCK, 2 * BLOCK), :] = jnp.zeros((2 * BLOCK, width), jnp.bfloat16)
 
     ones = jnp.ones((rows, LANES), jnp.bfloat16)
@@ -269,8 +280,8 @@
                 in_ring[way, hop, piece].wait_recv()
                 if hop < hops:
                     in_ring[way, hop + 1, piece] = ring_step(way, hop + 1, piece)
-        for send, ring, step, way in sends:
-            send(ring, step, way)
+            for send, ring, step, way in sends:
+                send(ring, step, way, piece)
         pass_plane(hop)
         finish(hop - 1)
     pass_plane(far - 1)
@@ -297,7 +308,7 @@
     ids = pltpu.VMEM((blocks, LANES), jnp.float32)
     return pl.pallas_call(
         functools.partial(kernel, depth, slabs),
-        out_shape=jax.ShapeDtypeStruct((rows, width), jnp.bfloat16),
+        out_shape=pltpu.VMEM((rows, width), jnp.bfloat16),
         in_specs=[pl.BlockSpec(memory_space=pl.ANY)] * 3,
         out_specs=pl.BlockSpec(memory_space=pltpu.VMEM),
         scratch_shapes=[

time: 83.7 us -> 79.2 us (0.946)
  Pallas kernels: 81.4 us -> 78.3 us
  local copies, waits for them, and re-layouts: 1.77 us -> 0.75 us
    pallas_call x1, Pallas kernels: 81.4 us -> 78.3 us  [local(): pl.pallas_call(functools.partial(kernel, depth, slabs), out_shape=pltpu.V...]
    unnamed x1, local copies, waits for them, and re-layouts: 1.77 us -> 0.75 us
where the time goes in v3:
time: 79.2 us; the launch traced here: 79 us
  Pallas kernels  78.3 us (99%)
    pallas_call x1, Pallas kernels, local(): pl.pallas_call(functools.partial(kernel, depth, slabs), out_shape=pltpu.V...  78.3 us

profile of v3, /device:TPU:24, one launch (start us, length us, event | category | flops | bytes accessed | tf_op | source)
XLA Modules:
  0.0 79.0 jit_solution(5057076740546361415)
XLA Ops:
  0.0 78.3 %shard_map.37 = bf16[256,768]{1,0:T(8,128)(2,1)S(1)} custom-call(bf16[256,768]{1,0:T(8,128)(2,1)} %embed.1, s32[1,256]{1,0:T(1,128)} %bitcast.1, s32[1,64,64]{2,1,0:T(8,128)} %pairs.1), custom_call_target="tpu_custom_call" | custom-call | tf_op jit(solution)/shard_map/pallas_call | solution.py:309
  78.3 0.7 copy.5

commit v4 on v3

--- a/solution.py
+++ b/solution.py
@@ -10,7 +10,7 @@
 BLOCK = 32
 WIDE = 4
 LANES = WIDE * BLOCK
-PIECES = 2
+PIECES = 3
 
 SHARPNESS = 60.0
 LEAKAGE = 0.3
@@ -195,7 +195,7 @@
         w = jnp.exp(scores * (SHARPNESS / width)) * factor
         return jnp.where(keep, w, 0.0).astype(jnp.bfloat16)
 
-    def against(theirs, halves, first=False):
+    def against(theirs, halves, first=False, last=False):
         scores = lax.dot_general(
             own[...], theirs, (((1,), (1,)), ((), ())), preferred_element_type=jnp.float32)
         ws = [
@@ -208,6 +208,9 @@
         if first:
             acc[...] = sums
             weight_sum[...] = totals
+        elif last:
+            scale = 1.0 / jnp.sum(weight_sum[...] + totals, axis=1, keepdims=True)
+            out[...] = ((acc[...] + sums) * scale).astype(out.dtype)
         else:
             acc[...] += sums
             weight_sum[...] += totals
@@ -241,12 +244,12 @@
 
     def pass_plane(hop):
         for way in (0, 1):
-            if hop and (way, hop) in in_plane:
+            if hop:
                 in_plane[way, hop].wait_recv()
-            if hop + 1 < far or (hop + 1 == far and way == 0):
-                in_plane[way, hop + 1] = copy(
-                    TILES, plane_sem.at[way, hop], planes.at[plane_at(way, hop)], planes.at[plane_at(way, hop + 1)],
-                    dev=node(1 - 2 * way, 0))
+            for further in (1, 2) if hop == hops and way == 0 else (1,):
+                in_plane[way, hop + further] = copy(
+                    TILES, plane_sem.at[way, hop + further - 1], planes.at[plane_at(way, hop)],
+                    planes.at[plane_at(way, hop + further)], dev=node(further * (1 - 2 * way), 0))
 
     def finish(step):
         blocks_in = {0: WIDE - 1 + 2, far - 1: 2 * WIDE, far: WIDE}.get(step, 2 * (WIDE - 1))
@@ -259,10 +262,14 @@
             ours = jnp.where(lane_part == 0, before, jnp.where(lane_part == 1, behind, -1.0))
             halves = [plane_half(0, 0), (topics, row_block == ours)]
         elif step == far:
+            in_plane[0, far].wait_recv()
             halves = [plane_half(-far, plane_at(0, far))]
         else:
+            if step == far - 1:
+                for way in (0, 1):
+                    in_plane[way, step].wait_recv()
             halves = [plane_half(-step, plane_at(0, step)), plane_half(step, plane_at(1, step))]
-        against(groups[pl.ds(step * rows, LANES * len(halves)), :], halves)
+        against(groups[pl.ds(step * rows, LANES * len(halves)), :], halves, last=step == far - 1)
 
     pass_plane(0)
     for hop in range(1, hops + 1):
@@ -276,22 +283,21 @@
             ring, by = rings[way * hops + hop - 1], 1 - 2 * way
             sends.append((picks(-by * hop, 0, range(WIDE)), ring, hop, way))
         for piece in range(PIECES):
+            if hop == 1 and piece == 1:
+                pass_plane(hop)
             for way in (0, 1):
                 in_ring[way, hop, piece].wait_recv()
                 if hop < hops:
                     in_ring[way, hop + 1, piece] = ring_step(way, hop + 1, piece)
+            if hop > 1 and piece == 0:
+                pass_plane(hop)
             for send, ring, step, way in sends:
                 send(ring, step, way, piece)
-        pass_plane(hop)
         finish(hop - 1)
-    pass_plane(far - 1)
     finish(hops)
-    pass_plane(far)
     finish(far)
     finish(far - 1)
 
-    total = jnp.sum(weight_sum[...], axis=1, keepdims=True)
-    out[...] = (acc[...] / total).astype(out.dtype)
     for way in (0, 1):
         await_bytes(send_sem.at[RING[way]], groups.at[pl.ds(0, hops * rows)])
     await_bytes(send_sem.at[BLOCKS], stage)

time: 79.2 us -> 78.2 us (0.987)
  Pallas kernels: 78.3 us -> 76.5 us
    pallas_call x1, Pallas kernels: 78.3 us -> 76.5 us  [local(): pl.pallas_call(functools.partial(kernel, depth, slabs), out_shape=pltpu.V...]
where the time goes in v4:
time: 78.2 us; the launch traced here: 77.3 us
  Pallas kernels  76.5 us (98%)
    pallas_call x1, Pallas kernels, local(): pl.pallas_call(functools.partial(kernel, depth, slabs), out_shape=pltpu.V...  76.5 us

profile of v4, /device:TPU:24, one launch (start us, length us, event | category | flops | bytes accessed | tf_op | source)
XLA Modules:
  0.0 77.3 jit_solution(4666294685251008685)
XLA Ops:
  0.0 76.5 %shard_map.37 = bf16[256,768]{1,0:T(8,128)(2,1)S(1)} custom-call(bf16[256,768]{1,0:T(8,128)(2,1)} %embed.1, s32[1,256]{1,0:T(1,128)} %bitcast.1, s32[1,64,64]{2,1,0:T(8,128)} %pairs.1), custom_call_target="tpu_custom_call" | custom-call | tf_op jit(solution)/shard_map/pallas_call | solution.py:315
  76.5 0.7 copy.5

commit v5 on v4

--- a/solution.py
+++ b/solution.py
@@ -84,6 +84,8 @@
     pl.semaphore_wait(barrier, len(takers) + 2)
 
     def part(piece):
+        if piece is None:
+            return pl.ds(0, width)
         return pl.ds(piece * (width // PIECES), width // PIECES)
 
     def ring_step(way, hop, piece):
@@ -162,8 +164,7 @@
 
     loads[2].wait()
     pick_own = picks(0, 0, range(WIDE))
-    for piece in range(PIECES):
-        pick_own(own, 0, 0, piece)
+    pick_own(own, 0, 0, None)
     groups[pl.ds(LANES + 2 * BLOCK, 2 * BLOCK), :] = jnp.zeros((2 * BLOCK, width), jnp.bfloat16)
 
     ones = jnp.ones((rows, LANES), jnp.bfloat16)
@@ -292,10 +293,13 @@
             if hop > 1 and piece == 0:
                 pass_plane(hop)
             for send, ring, step, way in sends:
-                send(ring, step, way, piece)
+                if hop == hops:
+                    send(ring, step, way, piece)
+                elif piece == PIECES - 1:
+                    send(ring, step, way, None)
         finish(hop - 1)
+    finish(far)
     finish(hops)
-    finish(far)
     finish(far - 1)
 
     for way in (0, 1):

time: 78.2 us -> 78 us (level)
  no operation moved by 1% of the time
where the time goes in v5:
time: 78 us; the launch traced here: 77.8 us
  Pallas kernels  77.1 us (99%)
    pallas_call x1, Pallas kernels, local(): pl.pallas_call(functools.partial(kernel, depth, slabs), out_shape=pltpu.V...  77.1 us

profile of v5, /device:TPU:24, one launch (start us, length us, event | category | flops | bytes accessed | tf_op | source)
XLA Modules:
  0.0 77.8 jit_solution(8713582316963587531)
XLA Ops:
  0.0 77.1 %shard_map.37 = bf16[256,768]{1,0:T(8,128)(2,1)S(1)} custom-call(bf16[256,768]{1,0:T(8,128)(2,1)} %embed.1, s32[1,256]{1,0:T(1,128)} %bitcast.1, s32[1,64,64]{2,1,0:T(8,128)} %pairs.1), custom_call_target="tpu_custom_call" | custom-call | tf_op jit(solution)/shard_map/pallas_call | solution.py:319
  77.1 0.7 copy.5
